TPU v7x, 512 devices: a whole 4x4x16 slice. The times are simulated.
512 devices in a mesh: dp: 128 (over x, z, y_lo), sub: 4 (over y_hi, core).
Axes of the slice: x: 4, y: 4 (y_hi: 2, y_lo: 2; y = y_hi * 2 + y_lo), z: 16, core: 2. Of those that a mesh axis runs over, the one named last changes fastest.
Arguments:
- visual_vectors: float32 [131072, 1152], P(('dp', 'sub')), may hold values from -1.2 to 1.2
- text_vectors: float32 [131072, 1152], P(('dp', 'sub')), may hold values from -1.2 to 1.2
- sharpness_factor: float32 [], replicated, may hold values from 1 to 3
- trainable_shift: float32 [], replicated, may hold values from -3 to -1
Outputs:
- visual_derivative_accumulated: float32 [131072, 1152], P(('dp', 'sub'))
- caption_grads: float32 [131072, 1152], P(('dp', 'sub'))
All inputs are finite; a program needn't handle non-finite values.
Results may differ from a plain program's by a relative error of at most 0.00011.
Values sent between devices are 32-bit elements; how exact they have to be, the bound alone decides.
A program may use at most 64 MiB of HBM per device.

v0:
```python
import jax
import jax.numpy as jnp
from jax import lax
from jax.sharding import PartitionSpec as P

STEPS = 4


def passed_along(shard, axis, by):
    length = lax.axis_size(axis)
    return lax.ppermute(shard, axis, [(i, (i + by) % length) for i in range(length)])


def local(visual_vectors, text_vectors, sharpness_factor, trainable_shift):
    highest_accuracy_mode = lax.Precision.HIGHEST
    rows = visual_vectors.shape[0]
    identity = jnp.eye(rows, dtype=jnp.float32)
    present_block = text_vectors
    visual_derivative_accumulated = jnp.zeros(visual_vectors.shape, jnp.float32)
    carried = jnp.zeros(text_vectors.shape, jnp.float32)
    for offset in range(STEPS):
        cosine_affinities = lax.dot_general(
            visual_vectors, present_block, (((1,), (1,)), ((), ())), precision=highest_accuracy_mode
        )
        cross_affinity_grid = sharpness_factor * cosine_affinities + trainable_shift
        objective_derivatives = jax.nn.sigmoid(cross_affinity_grid)
        if offset == 0:
            objective_derivatives = objective_derivatives - identity
        visual_derivative_accumulated = visual_derivative_accumulated + sharpness_factor * jnp.dot(
            objective_derivatives, present_block, precision=highest_accuracy_mode
        )
        objective_entries = sharpness_factor * lax.dot_general(
            objective_derivatives,
            visual_vectors,
            (((0,), (0,)), ((), ())),
            precision=highest_accuracy_mode,
        )
        carried = carried + objective_entries
        if offset + 1 < STEPS:
            carried = passed_along(carried, ("dp", "sub"), 1)
        if offset + 1 < STEPS:
            present_block = passed_along(present_block, ("dp", "sub"), 1)
    gathered = passed_along(carried, ("dp", "sub"), 1 - STEPS)
    return (visual_derivative_accumulated, gathered)


def solution(mesh):
    placed = (P(("dp", "sub"), None), P(("dp", "sub"), None), P(), P())
    return jax.shard_map(
        local,
        mesh=mesh,
        in_specs=placed,
        out_specs=(P(("dp", "sub"), None), P(("dp", "sub"), None)),
        check_vma=False,
    )
```

profile of v0, /device:TPU:1, one launch (start us, length us, event | category | flops | bytes accessed | tf_op | source)
XLA Modules:
  0.0 124.5 jit_solution(9106816965986105432)
XLA Ops:
  0.6 0.0 copy-start
  0.6 6.3 %collective-permute-start = (f32[256,1152]{1,0:T(8,128)}, f32[256,1152]{1,0:T(8,128)S(1)}, u32[]{:S(2)}, u32[]{:S(2)}) collective-permute-start(f32[256,1152]{1,0:T(8,128)} %param.5), channel_id=1, source_target_pairs={{0,1},{1,2},{2,3},{3,4},{4,5},{5,6},{6,7},{7,8},{8,9},{9,10},{10,1... | collective-permute-start | bytes 3538952 | tf_op jit(solution)/shard_map/ppermute | solution.py:11
  8.3 0.0 copy-done
  8.3 2.5 %fusion.22 = f32[256,256]{1,0:T(8,128)S(1)} fusion(f32[256,1152]{1,0:T(8,128)S(1)} %copy-done, f32[256,1152]{1,0:T(8,128)} %param.5, f32[]{:T(128)S(6)} %copy.8, f32[]{:T(128)S(6)} %copy.7), kind=kOutput, calls=%fused_computation.33 | convolution fusion | flops 906493952 | bytes 2621448 | tf_op jit(solution)/shard_map/dot_general | solution.py:22
  10.8 1.3 %convolution_multiply_fusion.3 = f32[256,1152]{1,0:T(8,128)S(1)} fusion(f32[256,256]{1,0:T(8,128)S(1)} %fusion.22, f32[256,1152]{1,0:T(8,128)S(1)} %copy-done, f32[]{:T(128)S(6)} %copy.7), kind=kOutput, calls=%fused_computation.4 | convolution fusion | flops 906264576 | bytes 2621444 | tf_op jit(solution)/shard_map/dot_general | solution.py:32
  12.1 1.9 %collective-permute-start.3 = (f32[256,1152]{1,0:T(8,128)S(1)}, f32[256,1152]{1,0:T(8,128)S(1)}, u32[]{:S(2)}, u32[]{:S(2)}) collective-permute-start(f32[256,1152]{1,0:T(8,128)S(1)} %convolution_multiply_fusion.3), channel_id=1, source_target_pairs={{0,1},{1,2},{2,3},{3,4},{4,5},{5,6},{6,7},{7,8},{8,9},{9,10},{10,1... | collective-permute-start | bytes 3538952 | tf_op jit(solution)/shard_map/ppermute | solution.py:11
  14.1 6.4 %collective-permute-done = f32[256,1152]{1,0:T(8,128)S(1)} collective-permute-done((f32[256,1152]{1,0:T(8,128)}, f32[256,1152]{1,0:T(8,128)S(1)}, u32[]{:S(2)}, u32[]{:S(2)}) %collective-permute-start) | collective-permute-done | bytes 1179680 | tf_op jit(solution)/shard_map/ppermute | solution.py:11
  20.4 5.8 %collective-permute-start.1 = (f32[256,1152]{1,0:T(8,128)S(1)}, f32[256,1152]{1,0:T(8,128)S(1)}, u32[]{:S(2)}, u32[]{:S(2)}) collective-permute-start(f32[256,1152]{1,0:T(8,128)S(1)} %collective-permute-done), channel_id=1, source_target_pairs={{0,1},{1,2},{2,3},{3,4},{4,5},{5,6},{6,7},{7,8},{8,9},{9,10},{10,1... | collective-permute-start | bytes 3538952 | tf_op jit(solution)/shard_map/ppermute | solution.py:11
  26.2 1.3 %fusion.17 = f32[256,256]{1,0:T(8,128)S(1)} fusion(f32[256,1152]{1,0:T(8,128)S(1)} %copy-done, f32[256,1152]{1,0:T(8,128)S(1)} %collective-permute-done, f32[]{:T(128)S(6)} %copy.8, f32[]{:T(128)S(6)} %copy.7), kind=kOutput, calls=%fused_computation.28 | convolution fusion | flops 906297344 | bytes 2621448 | tf_op jit(solution)/shard_map/dot_general | solution.py:22
  27.5 5.5 %collective-permute-done.3 = f32[256,1152]{1,0:T(8,128)S(1)} collective-permute-done((f32[256,1152]{1,0:T(8,128)S(1)}, f32[256,1152]{1,0:T(8,128)S(1)}, u32[]{:S(2)}, u32[]{:S(2)}) %collective-permute-start.3) | collective-permute-done | bytes 1179680 | tf_op jit(solution)/shard_map/ppermute | solution.py:11
  33.0 1.3 %fusion = f32[256,1152]{1,0:T(8,128)S(1)} fusion(f32[256,1152]{1,0:T(8,128)S(1)} %collective-permute-done.3, f32[256,256]{1,0:T(8,128)S(1)} %fusion.17, f32[256,1152]{1,0:T(8,128)S(1)} %copy-done, f32[]{:T(128)S(6)} %copy.7), kind=kOutput, calls=%fused_computation.3 | convolution fusion | flops 906559488 | bytes 3801092 | tf_op jit(solution)/shard_map/dot_general | solution.py:32
  34.3 5.9 %collective-permute-start.4 = (f32[256,1152]{1,0:T(8,128)S(1)}, f32[256,1152]{1,0:T(8,128)S(1)}, u32[]{:S(2)}, u32[]{:S(2)}) collective-permute-start(f32[256,1152]{1,0:T(8,128)S(1)} %fusion), channel_id=1, source_target_pairs={{0,1},{1,2},{2,3},{3,4},{4,5},{5,6},{6,7},{7,8},{8,9},{9,10},{10,1... | collective-permute-start | bytes 3538952 | tf_op jit(solution)/shard_map/ppermute | solution.py:11
  40.2 5.5 %collective-permute-done.1 = f32[256,1152]{1,0:T(8,128)S(1)} collective-permute-done((f32[256,1152]{1,0:T(8,128)S(1)}, f32[256,1152]{1,0:T(8,128)S(1)}, u32[]{:S(2)}, u32[]{:S(2)}) %collective-permute-start.1) | collective-permute-done | bytes 1179680 | tf_op jit(solution)/shard_map/ppermute | solution.py:11
  45.6 5.9 %collective-permute-start.2 = (f32[256,1152]{1,0:T(8,128)S(1)}, f32[256,1152]{1,0:T(8,128)S(1)}, u32[]{:S(2)}, u32[]{:S(2)}) collective-permute-start(f32[256,1152]{1,0:T(8,128)S(1)} %collective-permute-done.1), channel_id=1, source_target_pairs={{0,1},{1,2},{2,3},{3,4},{4,5},{5,6},{6,7},{7,8},{8,9},{9,10},{10,1... | collective-permute-start | bytes 3538952 | tf_op jit(solution)/shard_map/ppermute | solution.py:11
  51.5 1.3 %fusion.19 = f32[256,256]{1,0:T(8,128)S(1)} fusion(f32[256,1152]{1,0:T(8,128)S(1)} %copy-done, f32[256,1152]{1,0:T(8,128)S(1)} %collective-permute-done.1, f32[]{:T(128)S(6)} %copy.8, f32[]{:T(128)S(6)} %copy.7), kind=kOutput, calls=%fused_computation.30 | convolution fusion | flops 906297344 | bytes 2621448 | tf_op jit(solution)/shard_map/dot_general | solution.py:22
  52.8 1.3 %convolution_multiply_fusion.1 = f32[256,1152]{1,0:T(8,128)S(1)} fusion(f32[256,256]{1,0:T(8,128)S(1)} %fusion.19, f32[256,1152]{1,0:T(8,128)S(1)} %copy-done, f32[]{:T(128)S(6)} %copy.7), kind=kOutput, calls=%fused_computation.1 | convolution fusion | flops 906264576 | bytes 2621444 | tf_op jit(solution)/shard_map/dot_general | solution.py:32
  54.1 4.2 %collective-permute-done.4 = f32[256,1152]{1,0:T(8,128)S(1)} collective-permute-done((f32[256,1152]{1,0:T(8,128)S(1)}, f32[256,1152]{1,0:T(8,128)S(1)}, u32[]{:S(2)}, u32[]{:S(2)}) %collective-permute-start.4) | collective-permute-done | bytes 1179680 | tf_op jit(solution)/shard_map/ppermute | solution.py:11
  58.3 0.1 add.61
  58.4 5.9 %collective-permute-start.5 = (f32[256,1152]{1,0:T(8,128)S(1)}, f32[256,1152]{1,0:T(8,128)S(1)}, u32[]{:S(2)}, u32[]{:S(2)}) collective-permute-start(f32[256,1152]{1,0:T(8,128)S(1)} %add.61), channel_id=1, source_target_pairs={{0,1},{1,2},{2,3},{3,4},{4,5},{5,6},{6,7},{7,8},{8,9},{9,10},{10,1... | collective-permute-start | bytes 3538952 | tf_op jit(solution)/shard_map/ppermute | solution.py:11
  64.3 6.6 %collective-permute-done.2 = f32[256,1152]{1,0:T(8,128)S(1)} collective-permute-done((f32[256,1152]{1,0:T(8,128)S(1)}, f32[256,1152]{1,0:T(8,128)S(1)}, u32[]{:S(2)}, u32[]{:S(2)}) %collective-permute-start.2) | collective-permute-done | bytes 1179680 | tf_op jit(solution)/shard_map/ppermute | solution.py:11
  70.9 1.3 %fusion.21 = f32[256,256]{1,0:T(8,128)S(1)} fusion(f32[256,1152]{1,0:T(8,128)S(1)} %copy-done, f32[256,1152]{1,0:T(8,128)S(1)} %collective-permute-done.2, f32[]{:T(128)S(6)} %copy.8, f32[]{:T(128)S(6)} %copy.7), kind=kOutput, calls=%fused_computation.32 | convolution fusion | flops 906297344 | bytes 2621448 | tf_op jit(solution)/shard_map/dot_general | solution.py:22
  72.2 1.3 %convolution_multiply_fusion = f32[256,1152]{1,0:T(8,128)S(1)} fusion(f32[256,256]{1,0:T(8,128)S(1)} %fusion.21, f32[256,1152]{1,0:T(8,128)S(1)} %copy-done, f32[]{:T(128)S(6)} %copy.7), kind=kOutput, calls=%fused_computation | convolution fusion | flops 906264576 | bytes 2621444 | tf_op jit(solution)/shard_map/dot_general | solution.py:32
  73.5 0.0 copy-start.1
  73.5 10.1 %collective-permute-done.5 = f32[256,1152]{1,0:T(8,128)S(1)} collective-permute-done((f32[256,1152]{1,0:T(8,128)S(1)}, f32[256,1152]{1,0:T(8,128)S(1)}, u32[]{:S(2)}, u32[]{:S(2)}) %collective-permute-start.5) | collective-permute-done | bytes 1179680 | tf_op jit(solution)/shard_map/ppermute | solution.py:11
  83.5 0.1 add.62
  83.7 17.0 %collective-permute-start.6 = (f32[256,1152]{1,0:T(8,128)S(1)}, f32[256,1152]{1,0:T(8,128)S(1)}, u32[]{:S(2)}, u32[]{:S(2)}) collective-permute-start(f32[256,1152]{1,0:T(8,128)S(1)} %add.62), channel_id=1, source_target_pairs={{0,509},{1,510},{2,511},{3,0},{4,1},{5,2},{6,3},{7,4},{8,5},{9,6},... | collective-permute-start | bytes 3538952 | tf_op jit(solution)/shard_map/ppermute | solution.py:11
  100.7 0.0 copy-done.1
  100.7 1.2 fusion.23
  101.9 1.2 %convolution_add_fusion.2 = f32[256,1152]{1,0:T(8,128)S(1)} fusion(f32[256,1152]{1,0:T(8,128)S(1)} %fusion.23, f32[256,256]{1,0:T(8,128)S(1)} %fusion.17, f32[256,1152]{1,0:T(8,128)S(1)} %collective-permute-done), kind=kOutput, calls=%fused_computation.8 | convolution fusion | flops 906264576 | bytes 3801088 | tf_op jit(solution)/shard_map/dot_general | solution.py:29
  103.2 1.2 %convolution_add_fusion.1 = f32[256,1152]{1,0:T(8,128)S(1)} fusion(f32[256,1152]{1,0:T(8,128)S(1)} %convolution_add_fusion.2, f32[256,256]{1,0:T(8,128)S(1)} %fusion.19, f32[256,1152]{1,0:T(8,128)S(1)} %collective-permute-done.1), kind=kOutput, calls=%fused_computation.7 | convolution fusion | flops 906264576 | bytes 3801088 | tf_op jit(solution)/shard_map/dot_general | solution.py:29
  104.4 2.3 %fusion.1 = f32[256,1152]{1,0:T(8,128)} fusion(f32[256,1152]{1,0:T(8,128)S(1)} %convolution_add_fusion.1, f32[256,256]{1,0:T(8,128)S(1)} %fusion.21, f32[256,1152]{1,0:T(8,128)S(1)} %collective-permute-done.2, f32[]{:T(128)S(6)} %copy.7), kind=kOutput, calls=%fused_computation.6 | convolution fusion | flops 906559488 | bytes 3801092 | tf_op jit(solution)/shard_map/dot_general | solution.py:29
  106.7 16.7 %collective-permute-done.6 = f32[256,1152]{1,0:T(8,128)S(1)} collective-permute-done((f32[256,1152]{1,0:T(8,128)S(1)}, f32[256,1152]{1,0:T(8,128)S(1)}, u32[]{:S(2)}, u32[]{:S(2)}) %collective-permute-start.6) | collective-permute-done | bytes 1179680 | tf_op jit(solution)/shard_map/ppermute | solution.py:11
  123.4 1.0 copy.9
Async XLA Ops:
  0.6 7.7 %copy-start = (f32[256,1152]{1,0:T(8,128)S(1)}, f32[256,1152]{1,0:T(8,128)}, u32[]{:S(2)}) copy-start(f32[256,1152]{1,0:T(8,128)} %param.4) | copy-start | bytes 3538948
  0.6 19.8 %collective-permute-start = (f32[256,1152]{1,0:T(8,128)}, f32[256,1152]{1,0:T(8,128)S(1)}, u32[]{:S(2)}, u32[]{:S(2)}) collective-permute-start(f32[256,1152]{1,0:T(8,128)} %param.5), channel_id=1, source_target_pairs={{0,1},{1,2},{2,3},{3,4},{4,5},{5,6},{6,7},{7,8},{8,9},{9,10},{10,1... | collective-permute-start | bytes 3538952 | tf_op jit(solution)/shard_map/ppermute | solution.py:11
  12.1 20.8 %collective-permute-start.3 = (f32[256,1152]{1,0:T(8,128)S(1)}, f32[256,1152]{1,0:T(8,128)S(1)}, u32[]{:S(2)}, u32[]{:S(2)}) collective-permute-start(f32[256,1152]{1,0:T(8,128)S(1)} %convolution_multiply_fusion.3), channel_id=1, source_target_pairs={{0,1},{1,2},{2,3},{3,4},{4,5},{5,6},{6,7},{7,8},{8,9},{9,10},{10,1... | collective-permute-start | bytes 3538952 | tf_op jit(solution)/shard_map/ppermute | solution.py:11
  20.4 25.2 %collective-permute-start.1 = (f32[256,1152]{1,0:T(8,128)S(1)}, f32[256,1152]{1,0:T(8,128)S(1)}, u32[]{:S(2)}, u32[]{:S(2)}) collective-permute-start(f32[256,1152]{1,0:T(8,128)S(1)} %collective-permute-done), channel_id=1, source_target_pairs={{0,1},{1,2},{2,3},{3,4},{4,5},{5,6},{6,7},{7,8},{8,9},{9,10},{10,1... | collective-permute-start | bytes 3538952 | tf_op jit(solution)/shard_map/ppermute | solution.py:11
  34.3 24.0 %collective-permute-start.4 = (f32[256,1152]{1,0:T(8,128)S(1)}, f32[256,1152]{1,0:T(8,128)S(1)}, u32[]{:S(2)}, u32[]{:S(2)}) collective-permute-start(f32[256,1152]{1,0:T(8,128)S(1)} %fusion), channel_id=1, source_target_pairs={{0,1},{1,2},{2,3},{3,4},{4,5},{5,6},{6,7},{7,8},{8,9},{9,10},{10,1... | collective-permute-start | bytes 3538952 | tf_op jit(solution)/shard_map/ppermute | solution.py:11
  45.6 25.3 %collective-permute-start.2 = (f32[256,1152]{1,0:T(8,128)S(1)}, f32[256,1152]{1,0:T(8,128)S(1)}, u32[]{:S(2)}, u32[]{:S(2)}) collective-permute-start(f32[256,1152]{1,0:T(8,128)S(1)} %collective-permute-done.1), channel_id=1, source_target_pairs={{0,1},{1,2},{2,3},{3,4},{4,5},{5,6},{6,7},{7,8},{8,9},{9,10},{10,1... | collective-permute-start | bytes 3538952 | tf_op jit(solution)/shard_map/ppermute | solution.py:11
  58.4 25.2 %collective-permute-start.5 = (f32[256,1152]{1,0:T(8,128)S(1)}, f32[256,1152]{1,0:T(8,128)S(1)}, u32[]{:S(2)}, u32[]{:S(2)}) collective-permute-start(f32[256,1152]{1,0:T(8,128)S(1)} %add.61), channel_id=1, source_target_pairs={{0,1},{1,2},{2,3},{3,4},{4,5},{5,6},{6,7},{7,8},{8,9},{9,10},{10,1... | collective-permute-start | bytes 3538952 | tf_op jit(solution)/shard_map/ppermute | solution.py:11
  73.5 27.2 %copy-start.1 = (f32[256,1152]{1,0:T(8,128)S(1)}, f32[256,1152]{1,0:T(8,128)}, u32[]{:S(2)}) copy-start(f32[256,1152]{1,0:T(8,128)} %param.5) | copy-start | bytes 3538948
  83.7 39.8 %collective-permute-start.6 = (f32[256,1152]{1,0:T(8,128)S(1)}, f32[256,1152]{1,0:T(8,128)S(1)}, u32[]{:S(2)}, u32[]{:S(2)}) collective-permute-start(f32[256,1152]{1,0:T(8,128)S(1)} %add.62), channel_id=1, source_target_pairs={{0,509},{1,510},{2,511},{3,0},{4,1},{5,2},{6,3},{7,4},{8,5},{9,6},... | collective-permute-start | bytes 3538952 | tf_op jit(solution)/shard_map/ppermute | solution.py:11
where the time goes:
time: 125 us; the launch traced here: 124 us
  waiting for transfers between devices  54.9 us (44%)
  starting transfers between devices  48.7 us (39%)
  matrix products  17.4 us (14%)
  between operations  2.09 us (2%)
    ppermute x7, waiting for transfers between devices, passed_along(): lax.ppermute(shard, axis, [(i, (i + by) % length) for i in range(length)])  54.9 us
    ppermute x7, starting transfers between devices, passed_along(): lax.ppermute(shard, axis, [(i, (i + by) % length) for i in range(length)])  48.7 us
    dot_general x4, matrix products, local(): lax.dot_general(visual_vectors, present_block, (((1,), (1,)), ((), ())),...  6.33 us
    dot_general x4, matrix products, local(): jnp.dot(objective_derivatives, present_block, precision=highest_accuracy_...  6 us
    dot_general x4, matrix products, local(): lax.dot_general(objective_derivatives, visual_vectors, (((0,), (0,)), (()...  5.11 us
  transfers between devices with their start and end apart: 7, of which 7 were waited for; matrix products, arithmetic and copies ran while one was open for 14% of the time, Pallas kernels for 0%

commit v1 on v0

v1 whole, which is shorter than its diff:
```python
import functools

import jax
import jax.numpy as jnp
from jax import lax
from jax.experimental import pallas as pl
from jax.experimental.pallas import tpu as pltpu
from jax.sharding import PartitionSpec as P

MESH = pl.DeviceIdType.MESH
CHUNKS = 4
OWN_X, OWN_Y, PASSING, FAR, SIBLING, NEAR, NEAR_SIB, THROUGH, THROUGH_SIB = range(9)


def kernel(
    n_cols, n_z, sharp_ref, shift_ref, x_hbm, y_hbm, dx_hbm, dy_hbm, blocks, high, low, total,
    load_sem, near_send, near_recv, far_send, far_recv, relay_send, pass_send, pass_recv, thru_send, thru_recv,
    sib_send, sib_recv, share_send, share_recv, out_sem, late_sem,
):
    rows = x_hbm.shape[0]
    step = rows // CHUNKS
    dp, sub = lax.axis_index("dp"), lax.axis_index("sub")
    col, y, core = dp // 2, (sub // 2) * 2 + dp % 2, sub % 2
    z = col % n_z
    lower = y < 2
    edge = (y == 0) | (y == 3)
    shift_by = jnp.where(y == 0, n_cols - 1, jnp.where(y == 3, 1, 0))

    def at(y_, core_, by=0):
        c = (col + by) % n_cols
        return (c * 2 + y_ % 2, (y_ // 2) * 2 + core_)

    y_pair, y_far = y + 1 - 2 * (y % 2), 3 - y
    pair, across, sibling = at(y_pair, 1 - core), at(y_far, core), at(y, 1 - core)
    near_to = at(y_far, core, shift_by)
    far_to = at(y_pair, 1 - core, shift_by)
    relay_far_to = at(y, core, n_cols - shift_by)
    sends_far = lower == (core == 0)
    relays_far = ((y == 0) & (core == 0)) | ((y == 3) & (core == 1))
    holds_far = ((y == 1) & (core == 0)) | ((y == 2) & (core == 1))
    first, last = z == 0, z == n_z - 1

    barrier = pltpu.get_barrier_semaphore()

    def tell(to, when=None, sem=barrier):
        def go():
            pl.semaphore_signal(sem, inc=1, device_id=to, device_id_type=MESH)
        if when is None:
            go()
        else:
            pl.when(when)(go)

    is_ = lambda y_, core_: (y == y_) & (core == core_)
    one = lambda cond: jnp.where(cond, 1, 0)
    loads = [pltpu.make_async_copy(r, blocks.at[i], load_sem.at[i]) for i, r in enumerate((x_hbm, y_hbm))]
    for to in (pair, across, sibling):
        tell(to)
    tell(near_to, y == 0)
    tell(at(0, 0, n_cols - 1), is_(0, 0))
    tell(at(3, 1, n_cols - 1), is_(2, 0))
    tell(near_to, (y == 3) & ~last)
    tell(at(0, 0, 1), is_(1, 1) & ~last)
    tell(at(3, 1, 1), is_(3, 1) & ~last)
    tell(at(1, 1, n_cols - 1), is_(0, 0) & first)
    tell(at(3, 1, n_cols - 1), is_(3, 1) & first)
    for c in loads:
        c.start()
    back = one(y == 0) + one(is_(0, 0)) + one(is_(3, 1))
    arrivals = (
        3 + one(y == 3) + one(is_(3, 1)) + one(is_(0, 0)) + jnp.where(first, 0, back)
        + one((is_(1, 1) | is_(3, 1)) & last)
    )
    pl.semaphore_wait(barrier, arrivals)
    tell(near_to, (y == 3) & last, late_sem)
    tell(at(0, 0, 1), is_(1, 1) & last, late_sem)
    tell(at(3, 1, 1), is_(3, 1) & last, late_sem)
    for c in loads:
        c.wait()

    near_own = jnp.where(lower, OWN_X, OWN_Y)
    thru_own = 1 - near_own

    def part(slot, p):
        return blocks.at[slot, pl.ds(p * step, step)]

    def copy(src, dst, p, sems, to):
        return pltpu.make_async_remote_copy(
            src_ref=part(src, p), dst_ref=part(dst, p), send_sem=sems[0].at[p], recv_sem=sems[1].at[p],
            device_id=to, device_id_type=MESH,
        )

    passing = lambda p: copy(thru_own, PASSING, p, (pass_send, pass_recv), pair)
    near = lambda p: copy(near_own, NEAR, p, (near_send, near_recv), near_to)
    far = lambda p: copy(near_own, FAR, p, (far_send, far_recv), far_to)
    relay_far = lambda p: copy(PASSING, FAR, p, (relay_send, far_recv), relay_far_to)
    through = lambda p: copy(PASSING, THROUGH, p, (thru_send, thru_recv), across)
    share = lambda i, p: copy(
        jnp.where(i == 0, NEAR, THROUGH), jnp.where(i == 0, NEAR_SIB, THROUGH_SIB), p,
        (share_send.at[i], share_recv.at[i]), sibling,
    )
    swap = pltpu.make_async_remote_copy(
        src_ref=blocks.at[1 - core], dst_ref=blocks.at[SIBLING], send_sem=sib_send, recv_sem=sib_recv,
        device_id=sibling, device_id_type=MESH,
    )

    late = first & (back > 0)
    swap.start()
    for p in range(CHUNKS):
        passing(p).start()

    def start_near():
        for p in range(CHUNKS):
            near(p).start()

        @pl.when(sends_far)
        def _():
            for p in range(CHUNKS):
                far(p).start()

    held_back = first & (y == 0)
    pl.when(~held_back)(start_near)

    sharp, offset = sharp_ref[0], shift_ref[0]

    def split(v):
        hi = v.astype(jnp.bfloat16)
        return hi, (v - hi.astype(jnp.float32)).astype(jnp.bfloat16)

    for i in (OWN_X, OWN_Y):
        hi, lo = split(blocks[i])
        high[i] = hi
        low[i] = lo
    total[...] = jnp.zeros_like(total)

    def absorb(i, slot, at_row, size, own=None):
        w_hi, w_lo = split(blocks[slot, pl.ds(at_row, size)])
        nt = (((1,), (1,)), ((), ()))
        dot_t = lambda a, b: lax.dot_general(a, b, nt, preferred_element_type=jnp.float32)
        dot = lambda a, b: jnp.dot(a, b, preferred_element_type=jnp.float32)
        logits = dot_t(high[i], w_hi) + (dot_t(high[i], w_lo) + dot_t(low[i], w_hi))
        slopes = jax.nn.sigmoid(sharp * logits + offset)
        if own is not None:
            r = lax.broadcasted_iota(jnp.int32, slopes.shape, 0)
            c = lax.broadcasted_iota(jnp.int32, slopes.shape, 1)
            slopes = slopes - jnp.where((r == c) & own, 1.0, 0.0)
        s_hi, s_lo = split(sharp * slopes)
        total[i] += dot(s_hi, w_hi) + (dot(s_hi, w_lo) + dot(s_lo, w_hi))

    def own_and_sibling(j, carry):
        @pl.when(j == 2)
        def _():
            swap.wait()
        absorb(jnp.where(j == 2, 1 - core, j), jnp.where(j == 2, SIBLING, 1 - j), 0, rows, own=j < 2)
        return carry

    lax.fori_loop(0, 3, own_and_sibling, 0)

    for p in range(CHUNKS):
        passing(p).wait_recv()
        through(p).start()
        if p == 1:
            @pl.when(late)
            def _():
                pl.semaphore_wait(late_sem, back)
            pl.when(held_back)(start_near)
        if p > 0:
            @pl.when(relays_far)
            def _():
                relay_far(p - 1).start()

    @pl.when(relays_far)
    def _():
        relay_far(CHUNKS - 1).start()

    near_i = near_own
    thru_i = thru_own

    def arriving(p, carry):
        at_row = pl.multiple_of(p * step, step)
        near(p).wait_recv()
        share(0, p).start()
        through(p).wait_recv()
        share(1, p).start()

        @pl.when(p == CHUNKS - 1)
        def _():
            @pl.when(~holds_far)
            def _():
                for q in range(CHUNKS):
                    far(q).wait_recv()
            absorb(core, jnp.where(holds_far, PASSING, FAR), 0, rows)

        def pieces(k, carry):
            @pl.when(k >= 2)
            def _():
                share(k - 2, p).wait_recv()
            thru = k % 2
            absorb(
                jnp.where(thru == 0, near_i, thru_i),
                jnp.where(thru == 0, NEAR, THROUGH) + k // 2, at_row, step,
            )
            return carry

        lax.fori_loop(0, 4, pieces, 0)
        return carry

    lax.fori_loop(0, CHUNKS, arriving, 0)

    outs = [pltpu.make_async_copy(total.at[i], r, out_sem.at[i]) for i, r in enumerate((dx_hbm, dy_hbm))]
    for c in outs:
        c.start()
    for p in range(CHUNKS):
        passing(p).wait_send()
        near(p).wait_send()
        through(p).wait_send()
        share(0, p).wait_send()
        share(1, p).wait_send()

        @pl.when(sends_far)
        def _():
            far(p).wait_send()

        @pl.when(relays_far)
        def _():
            relay_far(p).wait_send()
    for c in outs:
        c.wait()


def solution(mesh):
    n_cols, n_z = mesh.shape["dp"] // 2, 16

    def local(visual_vectors, text_vectors, sharpness_factor, trainable_shift):
        rows, width = visual_vectors.shape
        shape = jax.ShapeDtypeStruct((rows, width), jnp.float32)
        smem = pl.BlockSpec(memory_space=pltpu.SMEM)
        hbm = pl.BlockSpec(memory_space=pl.ANY)
        dma = pltpu.SemaphoreType.DMA
        return pl.pallas_call(
            functools.partial(kernel, n_cols, n_z),
            out_shape=(shape, shape),
            in_specs=[smem, smem, hbm, hbm],
            out_specs=(hbm, hbm),
            scratch_shapes=[
                pltpu.VMEM((9, rows, width), jnp.float32),
                pltpu.VMEM((2, rows, width), jnp.bfloat16),
                pltpu.VMEM((2, rows, width), jnp.bfloat16),
                pltpu.VMEM((2, rows, width), jnp.float32),
                dma((2,)),
                *[dma((CHUNKS,))] * 9,
                dma, dma,
                dma((2, CHUNKS)), dma((2, CHUNKS)),
                dma((2,)),
                pltpu.SemaphoreType.REGULAR,
            ],
            compiler_params=pltpu.CompilerParams(
                collective_id=0, has_side_effects=True, vmem_limit_bytes=40 * 2**20
            ),
        )(sharpness_factor.reshape(1), trainable_shift.reshape(1), visual_vectors, text_vectors)

    split = P(("dp", "sub"), None)
    return jax.shard_map(
        local, mesh=mesh, in_specs=(split, split, P(), P()), out_specs=(split, split), check_vma=False,
    )
```

time: 125 us -> 87.1 us (0.70)
  Pallas kernels: 0 us -> 80.3 us
  waiting for transfers between devices: 54.9 us -> 0 us
  starting transfers between devices: 48.7 us -> 0 us
  matrix products: 17.4 us -> 0 us
  local copies, waits for them, and re-layouts: 1.03 us -> 4.56 us
    pallas_call x0 -> x1, Pallas kernels: none -> 80.3 us  [local(): pl.pallas_call(functools.partial(kernel, n_cols, n_z), out_shape=(shape,...]
    ppermute x7 -> x0, waiting for transfers between devices: 54.9 us -> none  [passed_along(): lax.ppermute(shard, axis, [(i, (i + by) % length) for i in range(length)])]
    ppermute x7 -> x0, starting transfers between devices: 48.7 us -> none  [passed_along(): lax.ppermute(shard, axis, [(i, (i + by) % length) for i in range(length)])]
    dot_general x12 -> x0, matrix products: 17.4 us -> none  [the longest x4 6.33 us: local(): lax.dot_general(visual_vectors, present_block, (((1,), (1,)), ((), ())),...]
    unnamed x5 -> x6, local copies, waits for them, and re-layouts: 1.03 us -> 4.56 us
  transfers between devices with their start and end apart: 7 -> 0, of which waited for: 7 -> 0; matrix products, arithmetic and copies ran while one was open for 14% -> 0% of each run, Pallas kernels for 0% -> 0%
where the time goes in v1:
time: 87.1 us; the launch traced here: 86.9 us
  Pallas kernels  80.3 us (92%)
  local copies, waits for them, and re-layouts  4.56 us (5%)
  between operations  1.94 us (2%)
    pallas_call x1, Pallas kernels, local(): pl.pallas_call(functools.partial(kernel, n_cols, n_z), out_shape=(shape,...  80.3 us
    unnamed x6, local copies, waits for them, and re-layouts  4.56 us

profile of v1, /device:TPU:1, one launch (start us, length us, event | category | flops | bytes accessed | tf_op | source)
XLA Modules:
  0.0 86.9 jit_solution(10264291981993149711)
XLA Ops:
  1.9 0.0 copy-start
  1.9 1.3 %copy-done = f32[256,1152]{1,0:T(8,128)S(1)} copy-done((f32[256,1152]{1,0:T(8,128)S(1)}, f32[256,1152]{1,0:T(8,128)}, u32[]{:S(2)}) %copy-start) | copy-done | bytes 1179672
  3.2 0.0 copy-start.1
  3.2 1.3 %copy-done.1 = f32[256,1152]{1,0:T(8,128)S(1)} copy-done((f32[256,1152]{1,0:T(8,128)S(1)}, f32[256,1152]{1,0:T(8,128)}, u32[]{:S(2)}) %copy-start.1) | copy-done | bytes 1179672
  4.5 80.3 %shard_map.59 = (f32[256,1152]{1,0:T(8,128)S(1)}, f32[256,1152]{1,0:T(8,128)S(1)}) custom-call(f32[1]{0:T(128)} %bitcast.2.sharp_ref, f32[1]{0:T(128)} %bitcast.3.shift_ref, f32[256,1152]{1,0:T(8,128)S(1)} %copy-done, f32[256,1152]{1,0:T(8,128)S(1)} %copy-done.1), custom_call_target="tpu_custom_call" | custom-call | tf_op jit(solution)/shard_map/pallas_call | solution.py:239
  84.8 1.0 %copy.10 = f32[256,1152]{1,0:T(8,128)} copy(f32[256,1152]{1,0:T(8,128)S(1)} %get-tuple-element.4) | data formatting | bytes 2359296
  85.8 1.0 %copy.11 = f32[256,1152]{1,0:T(8,128)} copy(f32[256,1152]{1,0:T(8,128)S(1)} %get-tuple-element.5) | data formatting | bytes 2359296
Async XLA Ops:
  1.9 1.3 %copy-start = (f32[256,1152]{1,0:T(8,128)S(1)}, f32[256,1152]{1,0:T(8,128)}, u32[]{:S(2)}) copy-start(f32[256,1152]{1,0:T(8,128)} %x_hbm.1) | copy-start | bytes 3538948
  3.2 1.3 %copy-start.1 = (f32[256,1152]{1,0:T(8,128)S(1)}, f32[256,1152]{1,0:T(8,128)}, u32[]{:S(2)}) copy-start(f32[256,1152]{1,0:T(8,128)} %y_hbm.1) | copy-start | bytes 3538948

commit v2 on v1

v2 whole, which is shorter than its diff:
```python
import functools

import jax
import jax.numpy as jnp
from jax import lax
from jax.experimental import pallas as pl
from jax.experimental.pallas import tpu as pltpu
from jax.sharding import PartitionSpec as P

MESH = pl.DeviceIdType.MESH
CHUNKS = 8
PIECE = 128
LAG = 3
LATE_AT = 2
FAR_AT = 5
OWN_X, OWN_Y, PASSING, FAR, SIBLING = range(5)
NEAR, THROUGH = range(2)


def kernel(
    n_cols, n_z, sharp_ref, shift_ref, x_hbm, y_hbm, total, blocks, pairs, high, low,
    load_sem, near_send, near_recv, far_send, far_recv, relay_send, pass_send, pass_recv, thru_send, thru_recv,
    sib_send, sib_recv, share_send, share_recv, late_sem,
):
    rows = x_hbm.shape[0]
    step = rows // CHUNKS
    dp, sub = lax.axis_index("dp"), lax.axis_index("sub")
    col, y, core = dp // 2, (sub // 2) * 2 + dp % 2, sub % 2
    z = col % n_z
    lower = y < 2
    edge = (y == 0) | (y == 3)
    shift_by = jnp.where(y == 0, n_cols - 1, jnp.where(y == 3, 1, 0))

    def at(y_, core_, by=0):
        c = (col + by) % n_cols
        return (c * 2 + y_ % 2, (y_ // 2) * 2 + core_)

    y_pair, y_far = y + 1 - 2 * (y % 2), 3 - y
    pair, across, sibling = at(y_pair, 1 - core), at(y_far, core), at(y, 1 - core)
    near_to = at(y_far, core, shift_by)
    far_to = at(y_pair, 1 - core, shift_by)
    relay_far_to = at(y, core, n_cols - shift_by)
    sends_far = lower == (core == 0)
    relays_far = ((y == 0) & (core == 0)) | ((y == 3) & (core == 1))
    holds_far = ((y == 1) & (core == 0)) | ((y == 2) & (core == 1))
    first, last = z == 0, z == n_z - 1

    barrier = pltpu.get_barrier_semaphore()

    def tell(to, when=None, sem=barrier):
        def go():
            pl.semaphore_signal(sem, inc=1, device_id=to, device_id_type=MESH)
        if when is None:
            go()
        else:
            pl.when(when)(go)

    is_ = lambda y_, core_: (y == y_) & (core == core_)
    one = lambda cond: jnp.where(cond, 1, 0)
    loads = [pltpu.make_async_copy(r, blocks.at[i], load_sem.at[i]) for i, r in enumerate((x_hbm, y_hbm))]
    for to in (pair, across, sibling):
        tell(to)
    tell(near_to, y == 0)
    tell(at(0, 0, n_cols - 1), is_(0, 0))
    tell(at(3, 1, n_cols - 1), is_(2, 0))
    tell(near_to, (y == 3) & ~last)
    tell(at(0, 0, 1), is_(1, 1) & ~last)
    tell(at(3, 1, 1), is_(3, 1) & ~last)
    tell(at(1, 1, n_cols - 1), is_(0, 0) & first)
    tell(at(3, 1, n_cols - 1), is_(3, 1) & first)
    for c in loads:
        c.start()
    back = one(y == 0) + one(is_(0, 0)) + one(is_(3, 1))
    arrivals = (
        3 + one(y == 3) + one(is_(3, 1)) + one(is_(0, 0)) + jnp.where(first, 0, back)
        + one((is_(1, 1) | is_(3, 1)) & last)
    )
    pl.semaphore_wait(barrier, arrivals)
    tell(near_to, (y == 3) & last, late_sem)
    tell(at(0, 0, 1), is_(1, 1) & last, late_sem)
    tell(at(3, 1, 1), is_(3, 1) & last, late_sem)
    for c in loads:
        c.wait()

    near_own = jnp.where(lower, OWN_X, OWN_Y)
    thru_own = 1 - near_own

    def part(slot, p):
        return blocks.at[slot, pl.ds(p * step, step)]

    def copy(src, dst, send, recv, to):
        return pltpu.make_async_remote_copy(
            src_ref=src, dst_ref=dst, send_sem=send, recv_sem=recv, device_id=to, device_id_type=MESH,
        )

    def passing(p):
        return copy(part(thru_own, p), part(PASSING, p), pass_send.at[p], pass_recv.at[p], pair)

    def near(p):
        return copy(part(near_own, p), pairs.at[NEAR, p, core], near_send.at[p], near_recv.at[p], near_to)

    def far(p):
        return copy(part(near_own, p), part(FAR, p), far_send.at[p], far_recv.at[p], far_to)

    def relay_far(p):
        return copy(part(PASSING, p), part(FAR, p), relay_send.at[p], far_recv.at[p], relay_far_to)

    def through(p):
        return copy(part(PASSING, p), pairs.at[THROUGH, p, core], thru_send.at[p], thru_recv.at[p], across)

    def share(i, p):
        here = pairs.at[i, p, core]
        return copy(here, here, share_send.at[i, p], share_recv.at[i, p], sibling)

    def shared(i, p):
        there = pairs.at[i, p, 1 - core]
        return copy(there, there, share_send.at[i, p], share_recv.at[i, p], sibling)

    swap = copy(blocks.at[1 - core], blocks.at[SIBLING], sib_send, sib_recv, sibling)

    late = first & (back > 0)
    held_back = first & (y == 0)
    for p in range(CHUNKS):
        passing(p).start()

    def start_near():
        for p in range(CHUNKS):
            near(p).start()

        @pl.when(sends_far)
        def _():
            for p in range(CHUNKS):
                far(p).start()

    pl.when(~held_back)(start_near)
    swap.start()

    sharp, offset = sharp_ref[0], shift_ref[0]

    def split(v):
        hi = v.astype(jnp.bfloat16)
        return hi, (v - hi.astype(jnp.float32)).astype(jnp.bfloat16)

    for i in (OWN_X, OWN_Y):
        hi, lo = split(blocks[i])
        high[i] = hi
        low[i] = lo
    total[...] = jnp.zeros_like(total)

    def dot_t(a, b):
        return lax.dot_general(a, b, (((1,), (1,)), ((), ())), preferred_element_type=jnp.float32)

    def absorb(i, w, diagonal=None):
        n = w.shape[0]
        w_hi, w_lo = split(w)
        both = dot_t(high[i], jnp.concatenate([w_hi, w_lo], 0))
        logits = both[:, :n] + (both[:, n:] + dot_t(low[i], w_hi))
        slopes = jax.nn.sigmoid(sharp * logits + offset)
        if diagonal is not None:
            r = lax.broadcasted_iota(jnp.int32, slopes.shape, 0)
            c = lax.broadcasted_iota(jnp.int32, slopes.shape, 1)
            slopes = slopes - jnp.where(r == c + diagonal, 1.0, 0.0)
        s_hi, s_lo = split(sharp * slopes)
        total[i] += jnp.dot(
            jnp.concatenate([s_hi, s_hi, s_lo], 1), jnp.concatenate([w_hi, w_lo, w_hi], 0),
            preferred_element_type=jnp.float32,
        )

    def absorb_block(i, slot, own=None):
        def one_piece(q, carry):
            at_row = pl.multiple_of(q * PIECE, PIECE)
            diagonal = None if own is None else at_row + jnp.where(own, 0, rows)
            absorb(i, blocks[slot, pl.ds(at_row, PIECE)], diagonal)
            return carry

        lax.fori_loop(0, rows // PIECE, one_piece, 0)

    def pair_rows(i, p, count):
        return pairs[i, pl.ds(p, count)].reshape(count * 2 * step, pairs.shape[-1])

    def receive_near(p):
        near(p).wait_recv()
        share(NEAR, p).start()

    group = PIECE // (2 * step)

    def absorb_near(p):
        for q in range(group):
            shared(NEAR, p + q).wait_recv()
        absorb(near_own, pair_rows(NEAR, p, group))

    def starting(j, carry):
        passing(j).wait_recv()
        through(j).start()

        @pl.when(late & (j == LATE_AT))
        def _():
            pl.semaphore_wait(late_sem, back)

        pl.when(held_back & (j == LATE_AT))(start_near)

        @pl.when(j == 2)
        def _():
            swap.wait_recv()

        absorb_block(jnp.where(j == 2, 1 - core, j), jnp.where(j == 2, SIBLING, 1 - j), own=j < 2)
        return carry

    lax.fori_loop(0, LAG, starting, 0)

    def flowing(p, carry):
        passing(p).wait_recv()
        through(p).start()

        @pl.when(late & (p == LATE_AT))
        def _():
            pl.semaphore_wait(late_sem, back)

        pl.when(held_back & (p == LATE_AT))(start_near)

        @pl.when(relays_far)
        def _():
            relay_far(p - LAG).start()

        receive_near(p - LAG)

        @pl.when((p - LAG) % group == group - 1)
        def _():
            absorb_near(p - LAG - (group - 1))

        return carry

    lax.fori_loop(LAG, CHUNKS, flowing, 0)

    for p in range(CHUNKS - LAG, CHUNKS):
        @pl.when(relays_far)
        def _():
            relay_far(p).start()

    def rest_of_near(p, carry):
        receive_near(p)

        @pl.when(p % group == group - 1)
        def _():
            absorb_near(p - (group - 1))

        return carry

    lax.fori_loop(CHUNKS - LAG, CHUNKS, rest_of_near, 0)

    def last_arrivals(p, carry):
        through(p).wait_recv()
        share(THROUGH, p).start()

        @pl.when(p == FAR_AT)
        def _():
            @pl.when(~holds_far)
            def _():
                for q in range(CHUNKS):
                    far(q).wait_recv()
            absorb_block(core, jnp.where(holds_far, PASSING, FAR))

        shared(THROUGH, p).wait_recv()
        absorb(thru_own, pair_rows(THROUGH, p, 1))
        return carry

    lax.fori_loop(0, CHUNKS, last_arrivals, 0)

    swap.wait_send()
    for p in range(CHUNKS):
        passing(p).wait_send()
        near(p).wait_send()
        through(p).wait_send()
        share(NEAR, p).wait_send()
        share(THROUGH, p).wait_send()

        @pl.when(sends_far)
        def _():
            far(p).wait_send()

        @pl.when(relays_far)
        def _():
            relay_far(p).wait_send()


def write_out(total, dx_hbm, dy_hbm, sem):
    copies = [pltpu.make_async_copy(total.at[i], r, sem.at[i]) for i, r in enumerate((dx_hbm, dy_hbm))]
    for c in copies:
        c.start()
    for c in copies:
        c.wait()


def solution(mesh):
    n_cols, n_z = mesh.shape["dp"] // 2, 16

    def local(visual_vectors, text_vectors, sharpness_factor, trainable_shift):
        rows, width = visual_vectors.shape
        shape = jax.ShapeDtypeStruct((rows, width), jnp.float32)
        smem = pl.BlockSpec(memory_space=pltpu.SMEM)
        vmem = pl.BlockSpec(memory_space=pltpu.VMEM)
        hbm = pl.BlockSpec(memory_space=pltpu.HBM)
        dma = pltpu.SemaphoreType.DMA
        total = pl.pallas_call(
            functools.partial(kernel, n_cols, n_z),
            out_shape=jax.ShapeDtypeStruct((2, rows, width), jnp.float32),
            in_specs=[smem, smem, hbm, hbm],
            out_specs=vmem,
            scratch_shapes=[
                pltpu.VMEM((5, rows, width), jnp.float32),
                pltpu.VMEM((2, CHUNKS, 2, rows // CHUNKS, width), jnp.float32),
                pltpu.VMEM((2, rows, width), jnp.bfloat16),
                pltpu.VMEM((2, rows, width), jnp.bfloat16),
                dma((2,)),
                *[dma((CHUNKS,))] * 9,
                dma, dma,
                dma((2, CHUNKS)), dma((2, CHUNKS)),
                pltpu.SemaphoreType.REGULAR,
            ],
            compiler_params=pltpu.CompilerParams(
                collective_id=0, has_side_effects=True, vmem_limit_bytes=40 * 2**20
            ),
        )(
            sharpness_factor.reshape(1), trainable_shift.reshape(1),
            pltpu.with_memory_space_constraint(visual_vectors, pltpu.HBM),
            pltpu.with_memory_space_constraint(text_vectors, pltpu.HBM),
        )
        return pl.pallas_call(
            write_out,
            out_shape=(shape, shape),
            in_specs=[vmem],
            out_specs=(hbm, hbm),
            scratch_shapes=[dma((2,))],
            compiler_params=pltpu.CompilerParams(vmem_limit_bytes=8 * 2**20),
        )(total)

    split = P(("dp", "sub"), None)
    return jax.shard_map(
        local, mesh=mesh, in_specs=(split, split, P(), P()), out_specs=(split, split), check_vma=False,
    )
```

time: 87.1 us -> 74 us (0.85)
  the two profiles are of different devices: /device:TPU:1 before, /device:TPU:9 now
where the time goes in v2:
time: 74 us; the launch traced here: 73.9 us
  Pallas kernels  71.9 us (97%)
  between operations  1.93 us (3%)
    pallas_call x1, Pallas kernels, local(): pl.pallas_call(functools.partial(kernel, n_cols, n_z), out_shape=jax.Shap...  70.5 us

profile of v2, /device:TPU:9, one launch (start us, length us, event | category | flops | bytes accessed | tf_op | source)
XLA Modules:
  0.0 73.9 jit_solution(1825982632363715141)
XLA Ops:
  1.9 70.5 %shard_map.59.total = f32[2,256,1152]{2,1,0:T(8,128)S(1)} custom-call(f32[1]{0:T(128)} %bitcast.2.sharp_ref, f32[1]{0:T(128)} %bitcast.3.shift_ref, f32[256,1152]{1,0:T(8,128)} %x_hbm.1, f32[256,1152]{1,0:T(8,128)} %y_hbm.1), custom_call_target="tpu_custom_call" | custom-call | tf_op jit(solution)/shard_map/pallas_call | solution.py:304
  72.5 1.4 %shard_map.60 = (f32[256,1152]{1,0:T(8,128)}, f32[256,1152]{1,0:T(8,128)}) custom-call(f32[2,256,1152]{2,1,0:T(8,128)S(1)} %shard_map.59.total), custom_call_target="tpu_custom_call" | custom-call | tf_op jit(solution)/shard_map/pallas_call | solution.py:328

commit v3 on v2

v3 whole, which is shorter than its diff:
```python
import functools

import jax
import jax.numpy as jnp
from jax import lax
from jax.experimental import pallas as pl
from jax.experimental.pallas import tpu as pltpu
from jax.sharding import PartitionSpec as P

MESH = pl.DeviceIdType.MESH
CHUNKS = 16
DOUBLES = CHUNKS // 2
PIECE = 128
LAG = 6
LATE_AT = 5
FAR_AT = 5
SENT_AT = 4
RELAY_AT = CHUNKS // 2 + 1
LOADS = 4
OWN_X, OWN_Y, PASSING, FAR, SIBLING = range(5)
NEAR, THROUGH = range(2)


def kernel(
    n_cols, n_z, sharp_ref, shift_ref, x_hbm, y_hbm, total, blocks, pairs, high, low,
    load_sem, near_send, near_recv, far_send, far_recv, relay_send, pass_send, pass_recv, thru_send, thru_recv,
    sib_send, sib_recv, share_send, near_share, thru_share, late_sem,
):
    rows = x_hbm.shape[0]
    step = rows // CHUNKS
    double = rows // DOUBLES
    dp, sub = lax.axis_index("dp"), lax.axis_index("sub")
    col, y, core = dp // 2, (sub // 2) * 2 + dp % 2, sub % 2
    z = col % n_z
    lower = y < 2
    edge = (y == 0) | (y == 3)
    shift_by = jnp.where(y == 0, n_cols - 1, jnp.where(y == 3, 1, 0))

    def at(y_, core_, by=0):
        c = (col + by) % n_cols
        return (c * 2 + y_ % 2, (y_ // 2) * 2 + core_)

    y_pair, y_far = y + 1 - 2 * (y % 2), 3 - y
    pair, across, sibling = at(y_pair, 1 - core), at(y_far, core), at(y, 1 - core)
    near_to = at(y_far, core, shift_by)
    far_to = at(y_pair, 1 - core, shift_by)
    relay_far_to = at(y, core, n_cols - shift_by)
    sends_far = lower == (core == 0)
    relays_far = ((y == 0) & (core == 0)) | ((y == 3) & (core == 1))
    holds_far = ((y == 1) & (core == 0)) | ((y == 2) & (core == 1))
    first, last = z == 0, z == n_z - 1

    barrier = pltpu.get_barrier_semaphore()

    def tell(to, when=None, sem=barrier):
        def go():
            pl.semaphore_signal(sem, inc=1, device_id=to, device_id_type=MESH)
        if when is None:
            go()
        else:
            pl.when(when)(go)

    is_ = lambda y_, core_: (y == y_) & (core == core_)
    one = lambda cond: jnp.where(cond, 1, 0)
    cuts = [pl.ds(q * (rows // LOADS), rows // LOADS) for q in range(LOADS)]
    loads = [
        pltpu.make_async_copy(r.at[cut], blocks.at[i, cut], load_sem.at[i])
        for i, r in enumerate((x_hbm, y_hbm)) for cut in cuts
    ]
    for to in (pair, across, sibling):
        tell(to)
    tell(near_to, y == 0)
    tell(at(0, 0, n_cols - 1), is_(0, 0))
    tell(at(3, 1, n_cols - 1), is_(2, 0))
    tell(near_to, (y == 3) & ~last)
    tell(at(0, 0, 1), is_(1, 1) & ~last)
    tell(at(3, 1, 1), is_(3, 1) & ~last)
    tell(at(1, 1, n_cols - 1), is_(0, 0) & first)
    tell(at(3, 1, n_cols - 1), is_(3, 1) & first)
    for c in loads:
        c.start()
    back = one(y == 0) + one(is_(0, 0)) + one(is_(3, 1))
    arrivals = (
        3 + one(y == 3) + one(is_(3, 1)) + one(is_(0, 0)) + jnp.where(first, 0, back)
        + one((is_(1, 1) | is_(3, 1)) & last)
    )
    pl.semaphore_wait(barrier, arrivals)
    tell(near_to, (y == 3) & last, late_sem)
    tell(at(0, 0, 1), is_(1, 1) & last, late_sem)
    tell(at(3, 1, 1), is_(3, 1) & last, late_sem)

    near_own = jnp.where(lower, OWN_X, OWN_Y)
    thru_own = 1 - near_own

    def part(slot, p):
        return blocks.at[slot, pl.ds(p * step, step)]

    def copy(src, dst, send, recv, to):
        return pltpu.make_async_remote_copy(
            src_ref=src, dst_ref=dst, send_sem=send, recv_sem=recv, device_id=to, device_id_type=MESH,
        )

    def passing(p, src):
        return copy(src.at[pl.ds(p * step, step)], part(PASSING, p), pass_send, pass_recv.at[p], pair)

    def near(d, src):
        src = src.at[pl.ds(d * double, double)]
        return copy(src, pairs.at[NEAR, d, core], near_send, near_recv.at[d], near_to)

    far = copy(blocks.at[near_own], blocks.at[FAR], far_send, far_recv, far_to)

    def relay_far(h):
        half = pl.ds(h * (rows // 2), rows // 2)
        return copy(blocks.at[PASSING, half], blocks.at[FAR, half], relay_send, far_recv, relay_far_to)

    def through(p):
        there = pairs.at[THROUGH, p // 2, core, pl.ds((p % 2) * step, step)]
        return copy(part(PASSING, p), there, thru_send, thru_recv.at[p // 2], across)

    def share(i, d):
        here = pairs.at[i, d, core]
        sem = near_share.at[d // group] if i == NEAR else thru_share.at[d]
        return copy(here, here, share_send.at[i], sem, sibling)

    def arrived(ref, sem):
        copy(ref, ref, far_send, sem, sibling).wait_recv()

    def sent(sem):
        copy(blocks.at[OWN_X], blocks.at[OWN_X], sem, far_recv, sibling).wait_send()

    group = PIECE // (2 * double)
    swap = copy(blocks.at[1 - core], blocks.at[SIBLING], sib_send, sib_recv, sibling)

    late = first & (back > 0)
    held_back = first & (y == 0)
    def start_near():
        @pl.when(lower)
        def _():
            for d in range(DOUBLES):
                near(d, x_hbm).start()

        @pl.when(~lower)
        def _():
            for d in range(DOUBLES):
                near(d, y_hbm).start()

    for mine, near_src, thru_src in ((lower, x_hbm, y_hbm), (~lower, y_hbm, x_hbm)):
        @pl.when(mine)
        def _():
            for p in range(CHUNKS):
                passing(p, thru_src).start()

                if p < DOUBLES:
                    @pl.when(~held_back)
                    def _():
                        near(p, near_src).start()

    for i, r in enumerate((x_hbm, y_hbm)):
        pltpu.make_async_copy(r, blocks.at[i], load_sem.at[i]).wait()

    far_at_once = last & (y == 3)
    pl.when(sends_far & far_at_once)(far.start)
    swap.start()

    sharp, offset = sharp_ref[0, 0], shift_ref[0, 0]

    def split(v):
        hi = v.astype(jnp.bfloat16)
        return hi, (v - hi.astype(jnp.float32)).astype(jnp.bfloat16)

    for i in (OWN_X, OWN_Y):
        hi, lo = split(blocks[i])
        high[i] = hi
        low[i] = lo
    total[...] = jnp.zeros_like(total)

    def dot_t(a, b):
        return lax.dot_general(a, b, (((1,), (1,)), ((), ())), preferred_element_type=jnp.float32)

    def absorb(i, w, diagonal=None):
        n = w.shape[0]
        w_hi, w_lo = split(w)
        both = dot_t(high[i], jnp.concatenate([w_hi, w_lo], 0))
        logits = both[:, :n] + (both[:, n:] + dot_t(low[i], w_hi))
        slopes = jax.nn.sigmoid(sharp * logits + offset)
        if diagonal is not None:
            r = lax.broadcasted_iota(jnp.int32, slopes.shape, 0)
            c = lax.broadcasted_iota(jnp.int32, slopes.shape, 1)
            slopes = slopes - jnp.where(r == c + diagonal, 1.0, 0.0)
        s_hi, s_lo = split(sharp * slopes)
        total[i] += jnp.dot(
            jnp.concatenate([s_hi, s_hi, s_lo], 1), jnp.concatenate([w_hi, w_lo, w_hi], 0),
            preferred_element_type=jnp.float32,
        )

    def absorb_piece(i, slot, q, own=None):
        at_row = pl.multiple_of(q * PIECE, PIECE)
        diagonal = None if own is None else at_row + jnp.where(own, 0, rows)
        absorb(i, blocks[slot, pl.ds(at_row, PIECE)], diagonal)

    pieces = rows // PIECE

    def pair_rows(i, d, count):
        return pairs[i, pl.ds(d, count)].reshape(count * 2 * double, pairs.shape[-1])

    def receive_near(d):
        arrived(pairs.at[NEAR, d, core], near_recv.at[d])
        share(NEAR, d).start()

    def absorb_near(d):
        arrived(pairs.at[NEAR, pl.ds(d, group), 1 - core], near_share.at[d // group])
        absorb(near_own, pair_rows(NEAR, d, group))

    def pass_on(p):
        arrived(part(PASSING, p), pass_recv.at[p])
        through(p).start()

        @pl.when(late & (p == LATE_AT))
        def _():
            pl.semaphore_wait(late_sem, back)

        pl.when(held_back & (p == LATE_AT))(start_near)

    def starting(j, carry):
        pass_on(j)

        @pl.when(j == 2 * pieces)
        def _():
            swap.wait_recv()

        which = j // pieces
        theirs = which == 2
        absorb_piece(
            jnp.where(theirs, 1 - core, which), jnp.where(theirs, SIBLING, 1 - which), j % pieces, own=~theirs
        )
        return carry

    lax.fori_loop(0, LAG, starting, 0)

    def take_near(d):
        receive_near(d)

        @pl.when((d > 0) & (d % group == 0))
        def _():
            absorb_near(d - group)

    def flowing(p, carry):
        pass_on(p)

        @pl.when(relays_far & (p == RELAY_AT))
        def _():
            relay_far(0).start()

        @pl.when((p - LAG) % 2 == 1)
        def _():
            take_near((p - LAG) // 2)

        return carry

    lax.fori_loop(LAG, CHUNKS, flowing, 0)

    @pl.when(relays_far)
    def _():
        relay_far(1).start()

    def rest_of_near(d, carry):
        take_near(d)
        return carry

    lax.fori_loop((CHUNKS - LAG) // 2, DOUBLES, rest_of_near, 0)
    absorb_near(DOUBLES - group)

    def absorb_through(d):
        arrived(pairs.at[THROUGH, d, 1 - core], thru_share.at[d])
        absorb(thru_own, pair_rows(THROUGH, d, 1))

    def last_arrivals(d, carry):
        arrived(pairs.at[THROUGH, d, core], thru_recv.at[d])
        share(THROUGH, d).start()
        pl.when(sends_far & ~far_at_once & (d == 0))(far.start)

        @pl.when((d == FAR_AT) & ~holds_far)
        def _():
            arrived(blocks.at[FAR], far_recv)

        @pl.when((d >= FAR_AT) & (d < FAR_AT + pieces))
        def _():
            absorb_piece(core, jnp.where(holds_far, PASSING, FAR), d - FAR_AT)

        @pl.when(d > 0)
        def _():
            absorb_through(d - 1)

        @pl.when(d == SENT_AT)
        def _():
            for sem in (sib_send, pass_send, near_send, share_send.at[NEAR]):
                sent(sem)

            pl.when(relays_far)(lambda: sent(relay_send))

        return carry

    lax.fori_loop(0, DOUBLES, last_arrivals, 0)
    absorb_through(DOUBLES - 1)
    sent(thru_send)
    sent(share_send.at[THROUGH])
    pl.when(sends_far)(lambda: sent(far_send))


def write_out(total, dx_hbm, dy_hbm, sem):
    part = dx_hbm.shape[0] // LOADS
    copies = [
        pltpu.make_async_copy(total.at[i, pl.ds(q * part, part)], r.at[pl.ds(q * part, part)], sem.at[i, q])
        for q in range(LOADS) for i, r in enumerate((dx_hbm, dy_hbm))
    ]
    for c in copies:
        c.start()
    for c in copies:
        c.wait()


def solution(mesh):
    n_cols, n_z = mesh.shape["dp"] // 2, 16

    def local(visual_vectors, text_vectors, sharpness_factor, trainable_shift):
        rows, width = visual_vectors.shape
        shape = jax.ShapeDtypeStruct((rows, width), jnp.float32)
        vmem = pl.BlockSpec(memory_space=pltpu.VMEM)
        hbm = pl.BlockSpec(memory_space=pltpu.HBM)
        dma = pltpu.SemaphoreType.DMA
        total = pl.pallas_call(
            functools.partial(kernel, n_cols, n_z),
            out_shape=jax.ShapeDtypeStruct((2, rows, width), jnp.float32),
            in_specs=[pl.BlockSpec(memory_space=pltpu.SMEM)] * 2 + [hbm, hbm],
            out_specs=vmem,
            scratch_shapes=[
                pltpu.VMEM((5, rows, width), jnp.float32),
                pltpu.VMEM((2, DOUBLES, 2, rows // DOUBLES, width), jnp.float32),
                pltpu.VMEM((2, rows, width), jnp.bfloat16),
                pltpu.VMEM((2, rows, width), jnp.bfloat16),
                dma((2,)),
                dma, dma((DOUBLES,)),
                dma, dma, dma,
                dma, dma((CHUNKS,)),
                dma, dma((DOUBLES,)),
                dma, dma,
                dma((2,)), dma((2 * rows // PIECE,)), dma((DOUBLES,)),
                pltpu.SemaphoreType.REGULAR,
            ],
            compiler_params=pltpu.CompilerParams(
                collective_id=0, has_side_effects=True, vmem_limit_bytes=40 * 2**20
            ),
        )(
            sharpness_factor.reshape(1, 1), trainable_shift.reshape(1, 1),
            *[pltpu.with_memory_space_constraint(v, pltpu.HBM) for v in (visual_vectors, text_vectors)]
        )
        return pl.pallas_call(
            write_out,
            out_shape=(shape, shape),
            in_specs=[vmem],
            out_specs=(hbm, hbm),
            scratch_shapes=[dma((2, LOADS))],
            compiler_params=pltpu.CompilerParams(vmem_limit_bytes=8 * 2**20),
        )(total)

    split = P(("dp", "sub"), None)
    return jax.shard_map(
        local, mesh=mesh, in_specs=(split, split, P(), P()), out_specs=(split, split), check_vma=False,
    )
```

time: 74 us -> 68.4 us (0.924)
  the two profiles are of different devices: /device:TPU:9 before, /device:TPU:1 now
where the time goes in v3:
time: 68.4 us; the launch traced here: 68.2 us
  Pallas kernels  66.3 us (97%)
  between operations  1.93 us (3%)
    pallas_call x1, Pallas kernels, local(): pl.pallas_call(functools.partial(kernel, n_cols, n_z), out_shape=jax.Shap...  64.8 us
    pallas_call x1, Pallas kernels, local(): pl.pallas_call(write_out, out_shape=(shape, shape), in_specs=[vmem], out_...  1.47 us

profile of v3, /device:TPU:1, one launch (start us, length us, event | category | flops | bytes accessed | tf_op | source)
XLA Modules:
  0.0 68.2 jit_solution(2986403194443060848)
XLA Ops:
  1.9 64.8 %shard_map.59.total = f32[2,256,1152]{2,1,0:T(8,128)S(1)} custom-call(f32[1,1]{1,0:T(1,128)} %bitcast.2.sharp_ref, f32[1,1]{1,0:T(1,128)} %bitcast.3.shift_ref, f32[256,1152]{1,0:T(8,128)} %x_hbm.1, f32[256,1152]{1,0:T(8,128)} %y_hbm.1), custom_call_target="tpu_custom_call" | custom-call | tf_op jit(solution)/shard_map/pallas_call | solution.py:331
  66.7 1.5 %shard_map.60 = (f32[256,1152]{1,0:T(8,128)}, f32[256,1152]{1,0:T(8,128)}) custom-call(f32[2,256,1152]{2,1,0:T(8,128)S(1)} %shard_map.59.total), custom_call_target="tpu_custom_call" | custom-call | tf_op jit(solution)/shard_map/pallas_call | solution.py:357

commit v4 on v3

--- a/solution.py
+++ b/solution.py
@@ -22,9 +22,9 @@
 
 
 def kernel(
-    n_cols, n_z, sharp_ref, shift_ref, x_hbm, y_hbm, total, blocks, pairs, high, low,
+    n_cols, n_z, sharp_ref, shift_ref, x_hbm, y_hbm, total, blocks, pairs, aside, high, low,
     load_sem, near_send, near_recv, far_send, far_recv, relay_send, pass_send, pass_recv, thru_send, thru_recv,
-    sib_send, sib_recv, share_send, near_share, thru_share, late_sem,
+    sib_send, sib_recv, share_send, near_share, thru_share, aside_send, aside_recv, late_sem,
 ):
     rows = x_hbm.shape[0]
     step = rows // CHUNKS
@@ -128,6 +128,10 @@
     def sent(sem):
         copy(blocks.at[OWN_X], blocks.at[OWN_X], sem, far_recv, sibling).wait_send()
 
+    last_rows = pl.ds(rows - double, double)
+    to_aside = copy(x_hbm.at[last_rows], aside, aside_send, aside_recv, across)
+    from_aside = copy(aside, pairs.at[THROUGH, DOUBLES - 1, 1 - core], aside_send, thru_recv.at[DOUBLES - 1], pair)
+    turn = jnp.where(first & (y == 0), DOUBLES - 1, 0)
     group = PIECE // (2 * double)
     swap = copy(blocks.at[1 - core], blocks.at[SIBLING], sib_send, sib_recv, sibling)
 
@@ -155,10 +159,11 @@
                     def _():
                         near(p, near_src).start()
 
+    pl.when(first & (y == 2))(to_aside.start)
     for i, r in enumerate((x_hbm, y_hbm)):
         pltpu.make_async_copy(r, blocks.at[i], load_sem.at[i]).wait()
 
-    far_at_once = last & (y == 3)
+    far_at_once = ~edge | (last & (y == 3))
     pl.when(sends_far & far_at_once)(far.start)
     swap.start()
 
@@ -213,7 +218,7 @@
 
     def pass_on(p):
         arrived(part(PASSING, p), pass_recv.at[p])
-        through(p).start()
+        pl.when(~(first & (y == 3)) | (p < CHUNKS - 2))(through(p).start)
 
         @pl.when(late & (p == LATE_AT))
         def _():
@@ -270,13 +275,22 @@
     lax.fori_loop((CHUNKS - LAG) // 2, DOUBLES, rest_of_near, 0)
     absorb_near(DOUBLES - group)
 
+    @pl.when(first & (y == 1))
+    def _():
+        arrived(aside, aside_recv)
+        from_aside.start()
+
+    def in_turn(d):
+        return (d + turn) % DOUBLES
+
     def absorb_through(d):
+        d = in_turn(d)
         arrived(pairs.at[THROUGH, d, 1 - core], thru_share.at[d])
         absorb(thru_own, pair_rows(THROUGH, d, 1))
 
     def last_arrivals(d, carry):
-        arrived(pairs.at[THROUGH, d, core], thru_recv.at[d])
-        share(THROUGH, d).start()
+        arrived(pairs.at[THROUGH, in_turn(d), core], thru_recv.at[in_turn(d)])
+        share(THROUGH, in_turn(d)).start()
         pl.when(sends_far & ~far_at_once & (d == 0))(far.start)
 
         @pl.when((d == FAR_AT) & ~holds_far)
@@ -302,7 +316,14 @@
 
     lax.fori_loop(0, DOUBLES, last_arrivals, 0)
     absorb_through(DOUBLES - 1)
-    sent(thru_send)
+    pl.when(~(first & (y == 3)))(lambda: sent(thru_send))
+
+    @pl.when(first & (y == 3))
+    def _():
+        most = blocks.at[PASSING, pl.ds(0, rows - double)]
+        copy(most, most, thru_send, far_recv, sibling).wait_send()
+
+    pl.when(first & ((y == 1) | (y == 2)))(to_aside.wait_send)
     sent(share_send.at[THROUGH])
     pl.when(sends_far)(lambda: sent(far_send))
 
@@ -336,6 +357,7 @@
             scratch_shapes=[
                 pltpu.VMEM((5, rows, width), jnp.float32),
                 pltpu.VMEM((2, DOUBLES, 2, rows // DOUBLES, width), jnp.float32),
+                pltpu.VMEM((rows // DOUBLES, width), jnp.float32),
                 pltpu.VMEM((2, rows, width), jnp.bfloat16),
                 pltpu.VMEM((2, rows, width), jnp.bfloat16),
                 dma((2,)),
@@ -345,6 +367,7 @@
                 dma, dma((DOUBLES,)),
                 dma, dma,
                 dma((2,)), dma((2 * rows // PIECE,)), dma((DOUBLES,)),
+                dma, dma,
                 pltpu.SemaphoreType.REGULAR,
             ],
             compiler_params=pltpu.CompilerParams(

time: 68.4 us -> 65.2 us (0.953)
  Pallas kernels: 66.3 us -> 63.1 us
    pallas_call x1, Pallas kernels: 64.8 us -> 61.6 us  [local(): pl.pallas_call(functools.partial(kernel, n_cols, n_z), out_shape=jax.Shap...]
where the time goes in v4:
time: 65.2 us; the launch traced here: 65 us
  Pallas kernels  63.1 us (97%)
  between operations  1.93 us (3%)
    pallas_call x1, Pallas kernels, local(): pl.pallas_call(functools.partial(kernel, n_cols, n_z), out_shape=jax.Shap...  61.6 us
    pallas_call x1, Pallas kernels, local(): pl.pallas_call(write_out, out_shape=(shape, shape), in_specs=[vmem], out_...  1.47 us

profile of v4, /device:TPU:1, one launch (start us, length us, event | category | flops | bytes accessed | tf_op | source)
XLA Modules:
  0.0 65.0 jit_solution(5865516523330340757)
XLA Ops:
  1.9 61.6 %shard_map.59.total = f32[2,256,1152]{2,1,0:T(8,128)S(1)} custom-call(f32[1,1]{1,0:T(1,128)} %bitcast.2.sharp_ref, f32[1,1]{1,0:T(1,128)} %bitcast.3.shift_ref, f32[256,1152]{1,0:T(8,128)} %x_hbm.1, f32[256,1152]{1,0:T(8,128)} %y_hbm.1), custom_call_target="tpu_custom_call" | custom-call | tf_op jit(solution)/shard_map/pallas_call | solution.py:352
  63.6 1.5 %shard_map.60 = (f32[256,1152]{1,0:T(8,128)}, f32[256,1152]{1,0:T(8,128)}) custom-call(f32[2,256,1152]{2,1,0:T(8,128)S(1)} %shard_map.59.total), custom_call_target="tpu_custom_call" | custom-call | tf_op jit(solution)/shard_map/pallas_call | solution.py:380

commit v5 on v4

--- a/solution.py
+++ b/solution.py
@@ -16,13 +16,41 @@
 FAR_AT = 5
 SENT_AT = 4
 RELAY_AT = CHUNKS // 2 + 1
-LOADS = 4
+LOADS = 1
+TILES = 3
 OWN_X, OWN_Y, PASSING, FAR, SIBLING = range(5)
 NEAR, THROUGH = range(2)
 
 
+def split(v):
+    hi = v.astype(jnp.bfloat16)
+    return hi, (v - hi.astype(jnp.float32)).astype(jnp.bfloat16)
+
+
+def dot_t(a, b):
+    return lax.dot_general(a, b, (((1,), (1,)), ((), ())), preferred_element_type=jnp.float32)
+
+
+def slopes_and_rows(high, low, w, sharp, offset, diagonal=None):
+    n = w.shape[0]
+    w_hi, w_lo = split(w)
+    both = dot_t(high, jnp.concatenate([w_hi, w_lo], 0))
+    logits = both[:, :n] + (both[:, n:] + dot_t(low, w_hi))
+    slopes = jax.nn.sigmoid(sharp * logits + offset)
+    if diagonal is not None:
+        r = lax.broadcasted_iota(jnp.int32, slopes.shape, 0)
+        c = lax.broadcasted_iota(jnp.int32, slopes.shape, 1)
+        slopes = slopes - jnp.where(r == c + diagonal, 1.0, 0.0)
+    s_hi, s_lo = split(sharp * slopes)
+    return jnp.concatenate([s_hi, s_hi, s_lo], 1), jnp.concatenate([w_hi, w_lo, w_hi], 0)
+
+
+def is_lower():
+    return lax.axis_index("sub") < 2
+
+
 def kernel(
-    n_cols, n_z, sharp_ref, shift_ref, x_hbm, y_hbm, total, blocks, pairs, aside, high, low,
+    n_cols, n_z, sharp_ref, shift_ref, x_hbm, y_hbm, total, last_ref, high, low, blocks, pairs, aside,
     load_sem, near_send, near_recv, far_send, far_recv, relay_send, pass_send, pass_recv, thru_send, thru_recv,
     sib_send, sib_recv, share_send, near_share, thru_share, aside_send, aside_recv, late_sem,
 ):
@@ -30,21 +58,23 @@
     step = rows // CHUNKS
     double = rows // DOUBLES
     dp, sub = lax.axis_index("dp"), lax.axis_index("sub")
-    col, y, core = dp // 2, (sub // 2) * 2 + dp % 2, sub % 2
-    z = col % n_z
-    lower = y < 2
+    col, y_low, y_high, core = lax.div(dp, 2), lax.rem(dp, 2), lax.div(sub, 2), lax.rem(sub, 2)
+    y = y_high * 2 + y_low
+    z = lax.rem(col, n_z)
+    lower = y_high == 0
     edge = (y == 0) | (y == 3)
-    shift_by = jnp.where(y == 0, n_cols - 1, jnp.where(y == 3, 1, 0))
-
-    def at(y_, core_, by=0):
-        c = (col + by) % n_cols
-        return (c * 2 + y_ % 2, (y_ // 2) * 2 + core_)
-
-    y_pair, y_far = y + 1 - 2 * (y % 2), 3 - y
-    pair, across, sibling = at(y_pair, 1 - core), at(y_far, core), at(y, 1 - core)
-    near_to = at(y_far, core, shift_by)
-    far_to = at(y_pair, 1 - core, shift_by)
-    relay_far_to = at(y, core, n_cols - shift_by)
+    after = jnp.where(col == n_cols - 1, 0, col + 1)
+    before = jnp.where(col == 0, n_cols - 1, col - 1)
+    ahead = jnp.where(y == 0, before, jnp.where(y == 3, after, col))
+    behind = jnp.where(y == 0, after, jnp.where(y == 3, before, col))
+
+    def at(y_low_, y_high_, core_, col_=col):
+        return (col_ * 2 + y_low_, y_high_ * 2 + core_)
+
+    pair, across, sibling = at(1 - y_low, y_high, 1 - core), at(1 - y_low, 1 - y_high, core), at(y_low, y_high, 1 - core)
+    near_to = at(1 - y_low, 1 - y_high, core, ahead)
+    far_to = at(1 - y_low, y_high, 1 - core, ahead)
+    relay_far_to = at(y_low, y_high, core, behind)
     sends_far = lower == (core == 0)
     relays_far = ((y == 0) & (core == 0)) | ((y == 3) & (core == 1))
     holds_far = ((y == 1) & (core == 0)) | ((y == 2) & (core == 1))
@@ -70,13 +100,13 @@
     for to in (pair, across, sibling):
         tell(to)
     tell(near_to, y == 0)
-    tell(at(0, 0, n_cols - 1), is_(0, 0))
-    tell(at(3, 1, n_cols - 1), is_(2, 0))
+    tell(at(0, 0, 0, before), is_(0, 0))
+    tell(at(1, 1, 1, before), is_(2, 0))
     tell(near_to, (y == 3) & ~last)
-    tell(at(0, 0, 1), is_(1, 1) & ~last)
-    tell(at(3, 1, 1), is_(3, 1) & ~last)
-    tell(at(1, 1, n_cols - 1), is_(0, 0) & first)
-    tell(at(3, 1, n_cols - 1), is_(3, 1) & first)
+    tell(at(0, 0, 0, after), is_(1, 1) & ~last)
+    tell(at(1, 1, 1, after), is_(3, 1) & ~last)
+    tell(at(1, 0, 1, before), is_(0, 0) & first)
+    tell(at(1, 1, 1, before), is_(3, 1) & first)
     for c in loads:
         c.start()
     back = one(y == 0) + one(is_(0, 0)) + one(is_(3, 1))
@@ -86,8 +116,8 @@
     )
     pl.semaphore_wait(barrier, arrivals)
     tell(near_to, (y == 3) & last, late_sem)
-    tell(at(0, 0, 1), is_(1, 1) & last, late_sem)
-    tell(at(3, 1, 1), is_(3, 1) & last, late_sem)
+    tell(at(0, 0, 0, after), is_(1, 1) & last, late_sem)
+    tell(at(1, 1, 1, after), is_(3, 1) & last, late_sem)
 
     near_own = jnp.where(lower, OWN_X, OWN_Y)
     thru_own = 1 - near_own
@@ -169,34 +199,15 @@
 
     sharp, offset = sharp_ref[0, 0], shift_ref[0, 0]
 
-    def split(v):
-        hi = v.astype(jnp.bfloat16)
-        return hi, (v - hi.astype(jnp.float32)).astype(jnp.bfloat16)
-
     for i in (OWN_X, OWN_Y):
         hi, lo = split(blocks[i])
         high[i] = hi
         low[i] = lo
     total[...] = jnp.zeros_like(total)
 
-    def dot_t(a, b):
-        return lax.dot_general(a, b, (((1,), (1,)), ((), ())), preferred_element_type=jnp.float32)
-
     def absorb(i, w, diagonal=None):
-        n = w.shape[0]
-        w_hi, w_lo = split(w)
-        both = dot_t(high[i], jnp.concatenate([w_hi, w_lo], 0))
-        logits = both[:, :n] + (both[:, n:] + dot_t(low[i], w_hi))
-        slopes = jax.nn.sigmoid(sharp * logits + offset)
-        if diagonal is not None:
-            r = lax.broadcasted_iota(jnp.int32, slopes.shape, 0)
-            c = lax.broadcasted_iota(jnp.int32, slopes.shape, 1)
-            slopes = slopes - jnp.where(r == c + diagonal, 1.0, 0.0)
-        s_hi, s_lo = split(sharp * slopes)
-        total[i] += jnp.dot(
-            jnp.concatenate([s_hi, s_hi, s_lo], 1), jnp.concatenate([w_hi, w_lo, w_hi], 0),
-            preferred_element_type=jnp.float32,
-        )
+        weights, parts = slopes_and_rows(high[i], low[i], w, sharp, offset, diagonal)
+        total[i] += jnp.dot(weights, parts, preferred_element_type=jnp.float32)
 
     def absorb_piece(i, slot, q, own=None):
         at_row = pl.multiple_of(q * PIECE, PIECE)
@@ -315,7 +326,8 @@
         return carry
 
     lax.fori_loop(0, DOUBLES, last_arrivals, 0)
-    absorb_through(DOUBLES - 1)
+    arrived(pairs.at[THROUGH, in_turn(DOUBLES - 1), 1 - core], thru_share.at[in_turn(DOUBLES - 1)])
+    last_ref[...] = pair_rows(THROUGH, in_turn(DOUBLES - 1), 1)
     pl.when(~(first & (y == 3)))(lambda: sent(thru_send))
 
     @pl.when(first & (y == 3))
@@ -328,16 +340,40 @@
     pl.when(sends_far)(lambda: sent(far_send))
 
 
-def write_out(total, dx_hbm, dy_hbm, sem):
-    part = dx_hbm.shape[0] // LOADS
-    copies = [
-        pltpu.make_async_copy(total.at[i, pl.ds(q * part, part)], r.at[pl.ds(q * part, part)], sem.at[i, q])
-        for q in range(LOADS) for i, r in enumerate((dx_hbm, dy_hbm))
-    ]
-    for c in copies:
-        c.start()
-    for c in copies:
-        c.wait()
+def finish(sharp_ref, shift_ref, total, last_ref, high, low, dx_hbm, dy_hbm, done, near_sem, thru_sem):
+    lower = is_lower()
+    thru_own = jnp.where(lower, OWN_Y, OWN_X)
+    width = done.shape[1]
+    tile = width // TILES
+
+    def out(go):
+        pl.when(lower)(lambda: go(dx_hbm, dy_hbm))
+        pl.when(~lower)(lambda: go(dy_hbm, dx_hbm))
+
+    def near_copy(near_hbm):
+        return pltpu.make_async_copy(total.at[1 - thru_own], near_hbm, near_sem)
+
+    def thru_copy(thru_hbm, q):
+        columns = pl.ds(q * tile, tile)
+        return pltpu.make_async_copy(done.at[:, columns], thru_hbm.at[:, columns], thru_sem.at[q])
+
+    out(lambda near_hbm, thru_hbm: near_copy(near_hbm).start())
+    weights, parts = slopes_and_rows(
+        high[thru_own], low[thru_own], last_ref[...], sharp_ref[0, 0], shift_ref[0, 0]
+    )
+    for q in range(TILES):
+        columns = slice(q * tile, (q + 1) * tile)
+        done[:, columns] = total[thru_own, :, columns] + jnp.dot(
+            weights, parts[:, columns], preferred_element_type=jnp.float32
+        )
+        out(lambda near_hbm, thru_hbm: thru_copy(thru_hbm, q).start())
+
+    def wait(near_hbm, thru_hbm):
+        for q in range(TILES):
+            thru_copy(thru_hbm, q).wait()
+        near_copy(near_hbm).wait()
+
+    out(wait)
 
 
 def solution(mesh):
@@ -346,20 +382,25 @@
     def local(visual_vectors, text_vectors, sharpness_factor, trainable_shift):
         rows, width = visual_vectors.shape
         shape = jax.ShapeDtypeStruct((rows, width), jnp.float32)
+        smem = pl.BlockSpec(memory_space=pltpu.SMEM)
         vmem = pl.BlockSpec(memory_space=pltpu.VMEM)
         hbm = pl.BlockSpec(memory_space=pltpu.HBM)
         dma = pltpu.SemaphoreType.DMA
-        total = pl.pallas_call(
+        scalars = sharpness_factor.reshape(1, 1), trainable_shift.reshape(1, 1)
+        sums = pl.pallas_call(
             functools.partial(kernel, n_cols, n_z),
-            out_shape=jax.ShapeDtypeStruct((2, rows, width), jnp.float32),
-            in_specs=[pl.BlockSpec(memory_space=pltpu.SMEM)] * 2 + [hbm, hbm],
-            out_specs=vmem,
+            out_shape=(
+                jax.ShapeDtypeStruct((2, rows, width), jnp.float32),
+                jax.ShapeDtypeStruct((2 * rows // DOUBLES, width), jnp.float32),
+                jax.ShapeDtypeStruct((2, rows, width), jnp.bfloat16),
+                jax.ShapeDtypeStruct((2, rows, width), jnp.bfloat16),
+            ),
+            in_specs=[smem, smem, hbm, hbm],
+            out_specs=(vmem,) * 4,
             scratch_shapes=[
                 pltpu.VMEM((5, rows, width), jnp.float32),
                 pltpu.VMEM((2, DOUBLES, 2, rows // DOUBLES, width), jnp.float32),
                 pltpu.VMEM((rows // DOUBLES, width), jnp.float32),
-                pltpu.VMEM((2, rows, width), jnp.bfloat16),
-                pltpu.VMEM((2, rows, width), jnp.bfloat16),
                 dma((2,)),
                 dma, dma((DOUBLES,)),
                 dma, dma, dma,
@@ -373,18 +414,15 @@
             compiler_params=pltpu.CompilerParams(
                 collective_id=0, has_side_effects=True, vmem_limit_bytes=40 * 2**20
             ),
-        )(
-            sharpness_factor.reshape(1, 1), trainable_shift.reshape(1, 1),
-            *[pltpu.with_memory_space_constraint(v, pltpu.HBM) for v in (visual_vectors, text_vectors)]
-        )
+        )(*scalars, *[pltpu.with_memory_space_constraint(v, pltpu.HBM) for v in (visual_vectors, text_vectors)])
         return pl.pallas_call(
-            write_out,
+            finish,
             out_shape=(shape, shape),
-            in_specs=[vmem],
+            in_specs=[smem, smem] + [vmem] * 4,
             out_specs=(hbm, hbm),
-            scratch_shapes=[dma((2, LOADS))],
-            compiler_params=pltpu.CompilerParams(vmem_limit_bytes=8 * 2**20),
-        )(total)
+            scratch_shapes=[pltpu.VMEM((rows, width), jnp.float32), dma, dma((TILES,))],
+            compiler_params=pltpu.CompilerParams(vmem_limit_bytes=12 * 2**20),
+        )(*scalars, *sums)
 
     split = P(("dp", "sub"), None)
     return jax.shard_map(

time: 65.2 us -> 64.6 us (level)
  no operation moved by 1% of the time
where the time goes in v5:
time: 64.6 us; the launch traced here: 64.5 us
  Pallas kernels  62.5 us (97%)
  between operations  1.93 us (3%)
    pallas_call x1, Pallas kernels, local(): pl.pallas_call(functools.partial(kernel, n_cols, n_z), out_shape=(jax.Sha...  60.6 us
    pallas_call x1, Pallas kernels, local(): pl.pallas_call(finish, out_shape=(shape, shape), in_specs=[smem, smem] +...  1.93 us

profile of v5, /device:TPU:1, one launch (start us, length us, event | category | flops | bytes accessed | tf_op | source)
XLA Modules:
  0.0 64.5 jit_solution(10628744247168701604)
XLA Ops:
  1.9 60.6 %shard_map.59 = (f32[2,256,1152]{2,1,0:T(8,128)S(1)}, f32[64,1152]{1,0:T(8,128)S(1)}, bf16[2,256,1152]{2,1,0:T(8,128)(2,1)S(1)}, bf16[2,256,1152]{2,1,0:T(8,128)(2,1)S(1)}) custom-call(f32[1,1]{1,0:T(1,128)} %bitcast.2.sharp_ref, f32[1,1]{1,0:T(1,128)} %bitcast.4.shift_ref, f32[256,1152]{1,0:T(8,128)} %x_hbm.1, f32[256,1152]{1,0:T(8,128)} %y_hbm.1), custom_call_target="tpu_custom_call" | custom-call | tf_op jit(solution)/shard_map/pallas_call | solution.py:390
  62.5 1.9 %shard_map.60 = (f32[256,1152]{1,0:T(8,128)}, f32[256,1152]{1,0:T(8,128)}) custom-call(f32[1,1]{1,0:T(1,128)} %bitcast.3.sharp_ref, f32[1,1]{1,0:T(1,128)} %bitcast.5.shift_ref, f32[2,256,1152]{2,1,0:T(8,128)S(1)} %get-tuple-element.6.total, f32[64,1152]{1,0:T(8,128)S(1)} %get-tuple-element.7.last_ref, bf16[2,256,1152]{2,1,0:T(8,128)(2,1)S(1)} %get-tuple-element.8.high, ...), custom_call_target="tpu_custom_call" | custom-call | tf_op jit(solution)/shard_map/pallas_call | solution.py:418

commit v6 on v5

--- a/solution.py
+++ b/solution.py
@@ -158,9 +158,16 @@
     def sent(sem):
         copy(blocks.at[OWN_X], blocks.at[OWN_X], sem, far_recv, sibling).wait_send()
 
-    last_rows = pl.ds(rows - double, double)
-    to_aside = copy(x_hbm.at[last_rows], aside, aside_send, aside_recv, across)
-    from_aside = copy(aside, pairs.at[THROUGH, DOUBLES - 1, 1 - core], aside_send, thru_recv.at[DOUBLES - 1], pair)
+    fourth = (lax.rem(z, 4) == 0) & ~first
+
+    def to_aside(size):
+        return copy(x_hbm.at[pl.ds(rows - size, size)], aside.at[pl.ds(0, size)], aside_send, aside_recv, across)
+
+    def from_aside(size):
+        there = pairs.at[THROUGH, DOUBLES - 1, 1 - core, pl.ds(double - size, size)]
+        return copy(aside.at[pl.ds(0, size)], there, aside_send, thru_recv.at[DOUBLES - 1], pair)
+
+    asides = ((first, double), (fourth, step))
     turn = jnp.where(first & (y == 0), DOUBLES - 1, 0)
     group = PIECE // (2 * double)
     swap = copy(blocks.at[1 - core], blocks.at[SIBLING], sib_send, sib_recv, sibling)
@@ -182,14 +189,15 @@
         @pl.when(mine)
         def _():
             for p in range(CHUNKS):
-                passing(p, thru_src).start()
-
                 if p < DOUBLES:
                     @pl.when(~held_back)
                     def _():
                         near(p, near_src).start()
 
-    pl.when(first & (y == 2))(to_aside.start)
+                passing(p, thru_src).start()
+
+    for here, size in asides:
+        pl.when(here & (y == 2))(to_aside(size).start)
     for i, r in enumerate((x_hbm, y_hbm)):
         pltpu.make_async_copy(r, blocks.at[i], load_sem.at[i]).wait()
 
@@ -229,7 +237,7 @@
 
     def pass_on(p):
         arrived(part(PASSING, p), pass_recv.at[p])
-        pl.when(~(first & (y == 3)) | (p < CHUNKS - 2))(through(p).start)
+        pl.when((y != 3) | (p < CHUNKS - jnp.where(first, 2, jnp.where(fourth, 1, 0))))(through(p).start)
 
         @pl.when(late & (p == LATE_AT))
         def _():
@@ -286,10 +294,11 @@
     lax.fori_loop((CHUNKS - LAG) // 2, DOUBLES, rest_of_near, 0)
     absorb_near(DOUBLES - group)
 
-    @pl.when(first & (y == 1))
-    def _():
-        arrived(aside, aside_recv)
-        from_aside.start()
+    for here, size in asides:
+        @pl.when(here & (y == 1))
+        def _():
+            arrived(aside.at[pl.ds(0, size)], aside_recv)
+            from_aside(size).start()
 
     def in_turn(d):
         return (d + turn) % DOUBLES
@@ -328,14 +337,15 @@
     lax.fori_loop(0, DOUBLES, last_arrivals, 0)
     arrived(pairs.at[THROUGH, in_turn(DOUBLES - 1), 1 - core], thru_share.at[in_turn(DOUBLES - 1)])
     last_ref[...] = pair_rows(THROUGH, in_turn(DOUBLES - 1), 1)
-    pl.when(~(first & (y == 3)))(lambda: sent(thru_send))
-
-    @pl.when(first & (y == 3))
-    def _():
-        most = blocks.at[PASSING, pl.ds(0, rows - double)]
-        copy(most, most, thru_send, far_recv, sibling).wait_send()
-
-    pl.when(first & ((y == 1) | (y == 2)))(to_aside.wait_send)
+    pl.when(~((first | fourth) & (y == 3)))(lambda: sent(thru_send))
+    for here, size in asides:
+        @pl.when(here & (y == 3))
+        def _():
+            most = blocks.at[PASSING, pl.ds(0, rows - size)]
+            copy(most, most, thru_send, far_recv, sibling).wait_send()
+
+        pl.when(here & ((y == 1) | (y == 2)))(to_aside(size).wait_send)
+
     sent(share_send.at[THROUGH])
     pl.when(sends_far)(lambda: sent(far_send))
 

time: 64.6 us -> 64.6 us (level)
  no operation moved by 1% of the time
where the time goes in v6:
time: 64.6 us; the launch traced here: 64.5 us
  Pallas kernels  62.5 us (97%)
  between operations  1.93 us (3%)
    pallas_call x1, Pallas kernels, local(): pl.pallas_call(functools.partial(kernel, n_cols, n_z), out_shape=(jax.Sha...  60.6 us
    pallas_call x1, Pallas kernels, local(): pl.pallas_call(finish, out_shape=(shape, shape), in_specs=[smem, smem] +...  1.93 us

profile of v6, /device:TPU:1, one launch (start us, length us, event | category | flops | bytes accessed | tf_op | source)
XLA Modules:
  0.0 64.5 jit_solution(14697960738334891896)
XLA Ops:
  1.9 60.6 %shard_map.59 = (f32[2,256,1152]{2,1,0:T(8,128)S(1)}, f32[64,1152]{1,0:T(8,128)S(1)}, bf16[2,256,1152]{2,1,0:T(8,128)(2,1)S(1)}, bf16[2,256,1152]{2,1,0:T(8,128)(2,1)S(1)}) custom-call(f32[1,1]{1,0:T(1,128)} %bitcast.2.sharp_ref, f32[1,1]{1,0:T(1,128)} %bitcast.4.shift_ref, f32[256,1152]{1,0:T(8,128)} %x_hbm.1, f32[256,1152]{1,0:T(8,128)} %y_hbm.1), custom_call_target="tpu_custom_call" | custom-call | tf_op jit(solution)/shard_map/pallas_call | solution.py:400
  62.5 1.9 %shard_map.60 = (f32[256,1152]{1,0:T(8,128)}, f32[256,1152]{1,0:T(8,128)}) custom-call(f32[1,1]{1,0:T(1,128)} %bitcast.3.sharp_ref, f32[1,1]{1,0:T(1,128)} %bitcast.5.shift_ref, f32[2,256,1152]{2,1,0:T(8,128)S(1)} %get-tuple-element.6.total, f32[64,1152]{1,0:T(8,128)S(1)} %get-tuple-element.7.last_ref, bf16[2,256,1152]{2,1,0:T(8,128)(2,1)S(1)} %get-tuple-element.8.high, ...), custom_call_target="tpu_custom_call" | custom-call | tf_op jit(solution)/shard_map/pallas_call | solution.py:428

commit v7 on v6

--- a/solution.py
+++ b/solution.py
@@ -335,8 +335,6 @@
         return carry
 
     lax.fori_loop(0, DOUBLES, last_arrivals, 0)
-    arrived(pairs.at[THROUGH, in_turn(DOUBLES - 1), 1 - core], thru_share.at[in_turn(DOUBLES - 1)])
-    last_ref[...] = pair_rows(THROUGH, in_turn(DOUBLES - 1), 1)
     pl.when(~((first | fourth) & (y == 3)))(lambda: sent(thru_send))
     for here, size in asides:
         @pl.when(here & (y == 3))
@@ -346,8 +344,10 @@
 
         pl.when(here & ((y == 1) | (y == 2)))(to_aside(size).wait_send)
 
+    pl.when(sends_far)(lambda: sent(far_send))
+    arrived(pairs.at[THROUGH, in_turn(DOUBLES - 1), 1 - core], thru_share.at[in_turn(DOUBLES - 1)])
+    last_ref[...] = pair_rows(THROUGH, in_turn(DOUBLES - 1), 1)
     sent(share_send.at[THROUGH])
-    pl.when(sends_far)(lambda: sent(far_send))
 
 
 def finish(sharp_ref, shift_ref, total, last_ref, high, low, dx_hbm, dy_hbm, done, near_sem, thru_sem):

time: 64.6 us -> 64.6 us (level)
  no operation moved by 1% of the time
where the time goes in v7:
time: 64.6 us; the launch traced here: 64.5 us
  Pallas kernels  62.5 us (97%)
  between operations  1.93 us (3%)
    pallas_call x1, Pallas kernels, local(): pl.pallas_call(functools.partial(kernel, n_cols, n_z), out_shape=(jax.Sha...  60.6 us
    pallas_call x1, Pallas kernels, local(): pl.pallas_call(finish, out_shape=(shape, shape), in_specs=[smem, smem] +...  1.94 us

profile of v7, /device:TPU:1, one launch (start us, length us, event | category | flops | bytes accessed | tf_op | source)
XLA Modules:
  0.0 64.5 jit_solution(5995166542707516619)
XLA Ops:
  1.9 60.6 %shard_map.59 = (f32[2,256,1152]{2,1,0:T(8,128)S(1)}, f32[64,1152]{1,0:T(8,128)S(1)}, bf16[2,256,1152]{2,1,0:T(8,128)(2,1)S(1)}, bf16[2,256,1152]{2,1,0:T(8,128)(2,1)S(1)}) custom-call(f32[1,1]{1,0:T(1,128)} %bitcast.2.sharp_ref, f32[1,1]{1,0:T(1,128)} %bitcast.4.shift_ref, f32[256,1152]{1,0:T(8,128)} %x_hbm.1, f32[256,1152]{1,0:T(8,128)} %y_hbm.1), custom_call_target="tpu_custom_call" | custom-call | tf_op jit(solution)/shard_map/pallas_call | solution.py:400
  62.5 1.9 %shard_map.60 = (f32[256,1152]{1,0:T(8,128)}, f32[256,1152]{1,0:T(8,128)}) custom-call(f32[1,1]{1,0:T(1,128)} %bitcast.3.sharp_ref, f32[1,1]{1,0:T(1,128)} %bitcast.5.shift_ref, f32[2,256,1152]{2,1,0:T(8,128)S(1)} %get-tuple-element.6.total, f32[64,1152]{1,0:T(8,128)S(1)} %get-tuple-element.7.last_ref, bf16[2,256,1152]{2,1,0:T(8,128)(2,1)S(1)} %get-tuple-element.8.high, ...), custom_call_target="tpu_custom_call" | custom-call | tf_op jit(solution)/shard_map/pallas_call | solution.py:428
